TPU v7x, 128 devices: a whole 4x4x4 slice. The times are simulated.
128 devices in a mesh: seq: 32 (over z_hi, x, y), head: 4 (over z_lo, core).
Axes of the slice: x: 4, y: 4, z: 4 (z_hi: 2, z_lo: 2; z = z_hi * 2 + z_lo), core: 2. Of those that a mesh axis runs over, the one named last changes fastest.
Arguments:
- queries: bfloat16 [65536, 2048], P('seq', 'head'), may hold values from -5 to 5
- key_field: bfloat16 [65536, 2048], P('seq', 'head'), may hold values from -5 to 5
- value_field: bfloat16 [65536, 2048], P('seq', 'head'), may hold values from -6 to 6
- out_grad: bfloat16 [65536, 2048], P('seq', 'head'), may hold values from -96 to 96
- prefix_keys: bfloat16 [64, 2048], P(None, 'head'), may hold values from -5 to 5
- prefix_values: bfloat16 [64, 2048], P(None, 'head'), may hold values from -6 to 6
Outputs:
- query_grad: bfloat16 [65536, 2048], P('seq', 'head')
- key_grad: bfloat16 [65536, 2048], P('seq', 'head')
- value_grad: bfloat16 [65536, 2048], P('seq', 'head')
- prefix_key_grad: float32 [64, 2048], P(None, 'head')
- prefix_value_grad: float32 [64, 2048], P(None, 'head')
All inputs are finite; a program needn't handle non-finite values.
Results may differ from a plain program's by a relative error of at most 0.0086.
Values may be sent and summed in bfloat16 or wider, within the bound.
A program may use at most 128 MiB of HBM per device.

v0:
```python
import math

import jax
import jax.numpy as jnp
from jax import lax
from jax.sharding import PartitionSpec as P

DH = 128
C = 1024
NPRE = 64


def passed_along(value, axis, steps):
    count = lax.axis_size(axis)
    leading, last = (max(0, -steps), min(count, count - steps))
    return lax.ppermute(value, axis, [(source, source + steps) for source in range(leading, last)])


def attend(query_blk, key_all, value_all, grad_blk, allowed):
    float_type = jnp.float32
    scaling = 1.0 / math.sqrt(query_blk.shape[-1])
    scores = (
        jnp.einsum("qbd,mbd->bqm", query_blk, key_all, preferred_element_type=float_type) * scaling
    )
    scores = jnp.where(allowed, scores, -jnp.inf)
    row_max = jnp.max(scores, axis=-1, keepdims=True)
    exp_terms = jnp.exp(scores - row_max)
    attn_probs = exp_terms / jnp.sum(exp_terms, axis=-1, keepdims=True)
    attn_round = attn_probs.astype(jnp.bfloat16)
    recomputed = jnp.einsum(
        "bqm,mbd->qbd", attn_round, value_all, preferred_element_type=float_type
    )
    delta_row = jnp.sum(grad_blk.astype(float_type) * recomputed, axis=-1)
    dprob = jnp.einsum("qbd,mbd->bqm", grad_blk, value_all, preferred_element_type=float_type)
    dscore = (scaling * attn_probs * (dprob - jnp.transpose(delta_row)[:, :, None])).astype(
        jnp.bfloat16
    )
    query_part = jnp.einsum("bqm,mbd->qbd", dscore, key_all, preferred_element_type=float_type)
    key_part = jnp.einsum("bqm,qbd->mbd", dscore, query_blk, preferred_element_type=float_type)
    value_part = jnp.einsum("bqm,qbd->mbd", attn_round, grad_blk, preferred_element_type=float_type)
    return (query_part, key_part, value_part)


def body(queries, key_field, value_field, out_grad, prefix_keys, prefix_values):
    length_here, width_here = queries.shape
    groups = width_here // (2 * DH)
    rows_here = length_here // C

    def split_heads(array, length):
        shaped = array.reshape(length, groups, 2, DH)
        return (shaped[:, :, 0], shaped[:, :, 1])

    q_even, q_odd = split_heads(queries, length_here)
    k_even, k_odd = split_heads(key_field, length_here)
    v_even, v_odd = split_heads(value_field, length_here)
    g_even, g_odd = split_heads(out_grad, length_here)
    pk_even, pk_odd = split_heads(prefix_keys, NPRE)
    pv_even, pv_odd = split_heads(prefix_values, NPRE)
    prior_pair = passed_along(
        jnp.stack([k_even[length_here - C :], v_even[length_here - C :]]), "seq", 1
    )
    k_ext = jnp.concatenate([prior_pair[0], k_even], axis=0)
    v_ext = jnp.concatenate([prior_pair[1], v_even], axis=0)
    offset_seq = lax.axis_index("seq") * length_here
    q_blk = min(512, C)
    pos_query = jnp.arange(q_blk, dtype=jnp.int32)[:, None]
    pos_key = jnp.arange(q_blk + C, dtype=jnp.int32)[None, :]
    prefix_on = jnp.ones((q_blk, NPRE), dtype=bool)

    def row_step(carry, block_idx):
        acc_k, acc_v, pre_k, pre_v = carry
        blk_start = block_idx * q_blk
        query_blk = lax.dynamic_slice_in_dim(q_even, blk_start, q_blk, 0)
        grad_blk = lax.dynamic_slice_in_dim(g_even, blk_start, q_blk, 0)
        key_blk = lax.dynamic_slice_in_dim(k_ext, blk_start, q_blk + C, 0)
        value_blk = lax.dynamic_slice_in_dim(v_ext, blk_start, q_blk + C, 0)
        window = (
            (pos_key >= pos_query + 1)
            & (pos_key <= pos_query + C)
            & (offset_seq + blk_start + pos_key - C >= 0)
        )
        allowed = jnp.concatenate([prefix_on, window], axis=1)
        query_part, key_part, value_part = attend(
            query_blk,
            jnp.concatenate([pk_even, key_blk], axis=0),
            jnp.concatenate([pv_even, value_blk], axis=0),
            grad_blk,
            allowed,
        )
        acc_k = lax.dynamic_update_slice_in_dim(
            acc_k,
            lax.dynamic_slice_in_dim(acc_k, blk_start, q_blk + C, 0) + key_part[NPRE:],
            blk_start,
            0,
        )
        acc_v = lax.dynamic_update_slice_in_dim(
            acc_v,
            lax.dynamic_slice_in_dim(acc_v, blk_start, q_blk + C, 0) + value_part[NPRE:],
            blk_start,
            0,
        )
        return (
            (acc_k, acc_v, pre_k + key_part[:NPRE], pre_v + value_part[:NPRE]),
            query_part.astype(jnp.bfloat16),
        )

    acc_zero = jnp.zeros((C + length_here, groups, DH), jnp.float32)
    pre_zero = jnp.zeros((NPRE, groups, DH), jnp.float32)
    blocks = jnp.arange(length_here // q_blk, dtype=jnp.int32)
    (acc_k, acc_v, pre_k_even, pre_v_even), dq_blocks = lax.scan(
        row_step, (acc_zero, acc_zero, pre_zero, pre_zero), blocks
    )
    returned = passed_along(jnp.stack([acc_k[:C], acc_v[:C]]), "seq", -1)
    dq_even = dq_blocks.reshape(length_here, groups, DH)
    dk_even = acc_k[C:].at[length_here - C :].add(returned[0]).astype(jnp.bfloat16)
    dv_even = acc_v[C:].at[length_here - C :].add(returned[1]).astype(jnp.bfloat16)

    def to_grid(array):
        return array.reshape(rows_here, C, groups, DH)

    col_q, col_k, col_v, col_g = (
        lax.all_to_all(to_grid(q_odd), "seq", split_axis=1, concat_axis=0, tiled=True),
        lax.all_to_all(to_grid(k_odd), "seq", split_axis=1, concat_axis=0, tiled=True),
        lax.all_to_all(to_grid(v_odd), "seq", split_axis=1, concat_axis=0, tiled=True),
        lax.all_to_all(to_grid(g_odd), "seq", split_axis=1, concat_axis=0, tiled=True),
    )
    rows_all, cols_here = (col_k.shape[0], col_k.shape[1])
    batch_size = cols_here * groups
    row_ids = jnp.arange(rows_all, dtype=jnp.int32)
    causal = row_ids[None, :] <= row_ids[:, None]
    allowed_col = jnp.concatenate([jnp.ones((rows_all, NPRE), dtype=bool), causal], axis=1)
    pk_wide = jnp.broadcast_to(pk_odd[:, None], (NPRE, cols_here, groups, DH)).reshape(
        NPRE, batch_size, DH
    )
    pv_wide = jnp.broadcast_to(pv_odd[:, None], (NPRE, cols_here, groups, DH)).reshape(
        NPRE, batch_size, DH
    )

    def flatten(array):
        return array.reshape(rows_all, batch_size, DH)

    query_part, key_part, value_part = attend(
        flatten(col_q),
        jnp.concatenate([pk_wide, flatten(col_k)], axis=0),
        jnp.concatenate([pv_wide, flatten(col_v)], axis=0),
        flatten(col_g),
        allowed_col,
    )
    shape_out = (rows_all, cols_here, groups, DH)
    pre_k_odd = key_part[:NPRE].reshape(NPRE, cols_here, groups, DH).sum(axis=1)
    pre_v_odd = value_part[:NPRE].reshape(NPRE, cols_here, groups, DH).sum(axis=1)
    dq_grid, dk_grid, dv_grid = (
        lax.all_to_all(
            query_part.reshape(shape_out).astype(jnp.bfloat16),
            "seq",
            split_axis=0,
            concat_axis=1,
            tiled=True,
        ),
        lax.all_to_all(
            key_part[NPRE:].reshape(shape_out).astype(jnp.bfloat16),
            "seq",
            split_axis=0,
            concat_axis=1,
            tiled=True,
        ),
        lax.all_to_all(
            value_part[NPRE:].reshape(shape_out).astype(jnp.bfloat16),
            "seq",
            split_axis=0,
            concat_axis=1,
            tiled=True,
        ),
    )
    total_k, total_v = lax.psum(
        (jnp.stack([pre_k_even, pre_k_odd], axis=2), jnp.stack([pre_v_even, pre_v_odd], axis=2)),
        "seq",
    )

    def merge_heads(even_part, odd_part):
        return jnp.stack([even_part, odd_part.reshape(length_here, groups, DH)], axis=2).reshape(
            length_here, width_here
        )

    query_grad = merge_heads(dq_even, dq_grid)
    key_grad = merge_heads(dk_even, dk_grid)
    value_grad = merge_heads(dv_even, dv_grid)
    prefix_key_grad = total_k.reshape(NPRE, width_here)
    prefix_value_grad = total_v.reshape(NPRE, width_here)
    return (query_grad, key_grad, value_grad, prefix_key_grad, prefix_value_grad)


def solution(mesh):
    return jax.shard_map(
        body,
        mesh=mesh,
        in_specs=(
            P("seq", "head"),
            P("seq", "head"),
            P("seq", "head"),
            P("seq", "head"),
            P(None, "head"),
            P(None, "head"),
        ),
        out_specs=(
            P("seq", "head"),
            P("seq", "head"),
            P("seq", "head"),
            P(None, "head"),
            P(None, "head"),
        ),
        check_vma=False,
    )
```

profile of v0, /device:TPU:0, one launch (start us, length us, event | category | flops | bytes accessed | tf_op | source)
XLA Modules:
  0.0 754.3 jit_solution(1252758910087470865)
XLA Ops:
  7.2 2.9 copy.87
  11.3 2.6 reshape_squeeze.14
  13.9 5.8 copy.105
  19.6 10.8 %all-to-all-start.2 = ((bf16[2,1024,2,128]{3,2,0,1:T(2,128)(2,1)}), bf16[2,1024,2,128]{3,2,0,1:T(2,128)(2,1)}, u32[]{:S(2)}, u32[]{:S(2)}) async-start(bf16[2,1024,2,128]{3,2,0,1:T(2,128)(2,1)} %copy.105), calls=%async_computation.2 | async-start | bytes 2097152 | tf_op jit(solution)/shard_map/all_to_all | solution.py:124
  30.5 3.9 copy.85
  34.4 3.1 slice_bitcast_fusion.4
  37.5 2.6 reshape_squeeze.12
  40.1 5.8 copy.98
  45.9 2.7 all-to-all-done.2
  48.7 7.1 all-to-all-start
  55.8 3.9 copy.84
  59.7 3.9 copy.90
  63.6 4.3 slice_bitcast_fusion.3
  68.0 2.6 reshape_squeeze.15
  70.6 5.8 copy.108
  76.4 9.9 %all-to-all-start.3 = ((bf16[2,1024,2,128]{3,2,0,1:T(2,128)(2,1)}), bf16[2,1024,2,128]{3,2,0,1:T(2,128)(2,1)}, u32[]{:S(2)}, u32[]{:S(2)}) async-start(bf16[2,1024,2,128]{3,2,0,1:T(2,128)(2,1)} %copy.108), calls=%async_computation.3 | async-start | bytes 2097152 | tf_op jit(solution)/shard_map/all_to_all | solution.py:125
  88.6 4.6 collective-permute-start
  94.1 3.8 copy.101
  97.8 6.4 all-to-all-done.3
  104.2 27.0 %all-to-all-start.1 = ((bf16[2,1024,2,128]{3,2,0,1:T(2,128)(2,1)}), bf16[2,1024,2,128]{3,2,0,1:T(2,128)(2,1)S(1)}, u32[]{:S(2)}, u32[]{:S(2)}) async-start(bf16[2,1024,2,128]{3,2,0,1:T(2,128)(2,1)} %copy.101), calls=%async_computation.1 | async-start | bytes 2097152 | tf_op jit(solution)/shard_map/all_to_all | solution.py:122
  143.0 2.2 all-to-all-done.1
  147.8 4.6 fusion.66
  152.7 3.2 fusion.40
  160.6 7.9 %all-to-all-start.4 = ((bf16[64,32,2,128]{3,1,2,0:T(8,128)(2,1)}), bf16[64,32,2,128]{3,1,2,0:T(8,128)(2,1)}, u32[]{:S(2)}, u32[]{:S(2)}) async-start(bf16[64,32,2,128]{3,1,2,0:T(8,128)(2,1)} %copy.111), calls=%async_computation.4 | async-start | bytes 2097152 | tf_op jit(solution)/shard_map/all_to_all | solution.py:153
  168.4 3.3 convolution_bitcast_fusion.3
  172.0 2.2 copy.117
  182.1 139.2 %while.24 = (s32[]{:T(128)}, f32[3072,2,128]{2,0,1:T(8,128)}, f32[3072,2,128]{2,0,1:T(8,128)}, f32[64,2,128]{2,0,1:T(8,128)}, f32[64,2,128]{2,0,1:T(8,128)}, /*i...) while((s32[]{:T(128)}, f32[3072,2,128]{2,0,1:T(8,128)}, ...), condition=%wide.region_4.5_spmd.clone.clone, body=%wide.region_0.4_spmd.clone.clone.sunk | while | flops 2545686528 | bytes 89619848 | solution.py:110
  190.0 6.3 fusion.104
  196.3 4.0 fusion.105
  200.2 2.5 fusion.106
  205.8 2.2 fusion.108
  212.5 3.9 fusion.107
  224.1 6.3 fusion.104
  230.4 4.0 fusion.105
  234.4 2.5 fusion.106
  240.0 2.2 fusion.108
  247.5 3.9 fusion.107
  259.1 6.3 fusion.104
  265.4 4.0 fusion.105
  269.3 2.5 fusion.106
  274.9 2.2 fusion.108
  282.5 3.9 fusion.107
  294.1 6.3 fusion.104
  300.4 4.0 fusion.105
  304.3 2.5 fusion.106
  309.9 2.2 fusion.108
  317.5 3.9 fusion.107
  321.4 2.4 slice_bitcast_fusion.7
  323.8 9.9 %all-to-all-start.6 = ((bf16[64,32,2,128]{3,2,1,0:T(2,128)(2,1)}), bf16[64,32,2,128]{3,2,1,0:T(2,128)(2,1)}, u32[]{:S(2)}, u32[]{:S(2)}) async-start(bf16[64,32,2,128]{3,2,1,0:T(2,128)(2,1)} %copy.117), calls=%async_computation.6 | async-start | bytes 2097152 | tf_op jit(solution)/shard_map/all_to_all | solution.py:167
  342.9 24.9 %all-to-all-done.6 = bf16[64,32,2,128]{3,2,1,0:T(2,128)(2,1)} async-done(((bf16[64,32,2,128]{3,2,1,0:T(2,128)(2,1)}), bf16[64,32,2,128]{3,2,1,0:T(2,128)(2,1)}, u32[]{:S(2)}, u32[]{:S(2)}) %all-to-all-start.6) | async-done | bytes 1048608 | tf_op jit(solution)/shard_map/all_to_all | solution.py:167
  367.8 12.0 %all-to-all-start.5 = ((bf16[64,32,2,128]{3,2,1,0:T(2,128)(2,1)}), bf16[64,32,2,128]{3,2,1,0:T(2,128)(2,1)}, u32[]{:S(2)}, u32[]{:S(2)}) async-start(bf16[64,32,2,128]{3,2,1,0:T(2,128)(2,1)} %copy.114), calls=%async_computation.5 | async-start | bytes 2097152 | tf_op jit(solution)/shard_map/all_to_all | solution.py:160
  379.8 3.3 slice.219
  388.0 2.7 slice.174
  393.7 2.3 copy.112
  396.0 2.4 copy.118
  398.4 2.5 copy.115
  402.4 3.9 copy.113
  406.3 3.9 copy.122
  410.3 3.1 fusion.44
  414.8 12.8 %copy.119 = bf16[2048,2,2,128]{3,2,1,0:T(2,128)(2,1)S(1)} copy(bf16[2048,2,2,128]{3,0,1,2:T(8,128)(2,1)S(1)} %pad_maximum_fusion.15) | data formatting | bytes 4194304 | tf_op jit(solution)/shard_map/stack | solution.py:181
  427.6 2.2 reshape.202
  431.2 12.8 %copy.116 = bf16[2048,2,2,128]{3,2,1,0:T(2,128)(2,1)S(1)} copy(bf16[2048,2,2,128]{3,0,1,2:T(8,128)(2,1)S(1)} %pad_maximum_fusion.14) | data formatting | bytes 4194304 | tf_op jit(solution)/shard_map/stack | solution.py:181
  444.0 2.2 reshape.200
  446.3 297.8 %all-reduce.5.cloned.1.call-done = (f32[64,512]{1,0:T(8,128)}, f32[64,512]{1,0:T(8,128)}) async-done(((f32[64,512]{1,0:T(8,128)}, f32[64,512]{1,0:T(8,128)}), (f32[64,512]{1,0:T(8,128)}, f32[64,512]{1,0:T(8,128)})) %all-reduce.5.cloned.1.call-update) | async-done | bytes 262160 | tf_op jit(solution)/shard_map/psum | solution.py:175
  (211 shorter events, 116.9 us)
Async XLA Ops:
  19.6 29.0 %all-to-all-start.2 = ((bf16[2,1024,2,128]{3,2,0,1:T(2,128)(2,1)}), bf16[2,1024,2,128]{3,2,0,1:T(2,128)(2,1)}, u32[]{:S(2)}, u32[]{:S(2)}) async-start(bf16[2,1024,2,128]{3,2,0,1:T(2,128)(2,1)} %copy.105), calls=%async_computation.2 | async-start | bytes 2097152 | tf_op jit(solution)/shard_map/all_to_all | solution.py:124
  48.7 27.7 %all-to-all-start = ((bf16[2,1024,2,128]{3,2,0,1:T(2,128)(2,1)}), bf16[2,1024,2,128]{3,2,0,1:T(2,128)(2,1)}, u32[]{:S(2)}, u32[]{:S(2)}) async-start(bf16[2,1024,2,128]{3,2,0,1:T(2,128)(2,1)} %copy.98), calls=%async_computation | async-start | bytes 2097152 | tf_op jit(solution)/shard_map/all_to_all | solution.py:123
  76.4 27.9 %all-to-all-start.3 = ((bf16[2,1024,2,128]{3,2,0,1:T(2,128)(2,1)}), bf16[2,1024,2,128]{3,2,0,1:T(2,128)(2,1)}, u32[]{:S(2)}, u32[]{:S(2)}) async-start(bf16[2,1024,2,128]{3,2,0,1:T(2,128)(2,1)} %copy.108), calls=%async_computation.3 | async-start | bytes 2097152 | tf_op jit(solution)/shard_map/all_to_all | solution.py:125
  86.2 7.0 copy-start.22
  86.3 7.0 copy-start.23
  87.5 5.8 copy-start.11
  88.6 85.6 %collective-permute-start = (bf16[2,1024,2,128]{1,3,2,0:T(8,128)(2,1)}, bf16[2,1024,2,128]{1,3,2,0:T(8,128)(2,1)}, u32[]{:S(2)}, u32[]{:S(2)}) collective-permute-start(bf16[2,1024,2,128]{1,3,2,0:T(8,128)(2,1)} %pad_maximum_fusion.22), channel_id=1, source_target_pairs={{0,4},{4,8},{8,12},{12,16},{16,20},{20,24},{24,28},{28,32},{32,36}... | collective-permute-start | bytes 3145736 | tf_op jit(solution)/shard_map/ppermute | solution.py:16
  104.2 41.0 %all-to-all-start.1 = ((bf16[2,1024,2,128]{3,2,0,1:T(2,128)(2,1)}), bf16[2,1024,2,128]{3,2,0,1:T(2,128)(2,1)S(1)}, u32[]{:S(2)}, u32[]{:S(2)}) async-start(bf16[2,1024,2,128]{3,2,0,1:T(2,128)(2,1)} %copy.101), calls=%async_computation.1 | async-start | bytes 2097152 | tf_op jit(solution)/shard_map/all_to_all | solution.py:122
  146.5 5.9 copy-start.5
  147.8 4.8 copy-start.15
  152.6 3.3 copy-start.16
  152.7 3.3 copy-start.24
  155.9 2.0 copy-start.17
  155.9 2.0 copy-start.18
  157.9 1.0 copy-start.19
  160.6 163.2 %all-to-all-start.4 = ((bf16[64,32,2,128]{3,1,2,0:T(8,128)(2,1)}), bf16[64,32,2,128]{3,1,2,0:T(8,128)(2,1)}, u32[]{:S(2)}, u32[]{:S(2)}) async-start(bf16[64,32,2,128]{3,1,2,0:T(8,128)(2,1)} %copy.111), calls=%async_computation.4 | async-start | bytes 2097152 | tf_op jit(solution)/shard_map/all_to_all | solution.py:153
  171.8 2.4 copy-start.12
  175.5 1.6 copy-start.4
  196.3 4.0 copy-start.3
  196.3 7.6 %slice-start = ((s8[6553600]{0:T(1024)(128)(4,1)}), s8[4194304]{0:T(1024)(128)(4,1)S(1)}, s32[]{:S(2)}) async-start(s8[6553600]{0:T(1024)(128)(4,1)} %bitcast.191), calls=%async_computation.8 | async-start | bytes 8388608 | tf_op jit(solution)/shard_map/while
  200.2 3.6 slice-start.1
  230.4 4.0 copy-start.3
  230.4 7.6 %slice-start = ((s8[6553600]{0:T(1024)(128)(4,1)}), s8[4194304]{0:T(1024)(128)(4,1)S(1)}, s32[]{:S(2)}) async-start(s8[6553600]{0:T(1024)(128)(4,1)} %bitcast.191), calls=%async_computation.8 | async-start | bytes 8388608 | tf_op jit(solution)/shard_map/while
  234.4 3.6 slice-start.1
  265.4 4.0 copy-start.3
  265.4 7.6 %slice-start = ((s8[6553600]{0:T(1024)(128)(4,1)}), s8[4194304]{0:T(1024)(128)(4,1)S(1)}, s32[]{:S(2)}) async-start(s8[6553600]{0:T(1024)(128)(4,1)} %bitcast.191), calls=%async_computation.8 | async-start | bytes 8388608 | tf_op jit(solution)/shard_map/while
  269.3 3.6 slice-start.1
  300.4 4.0 copy-start.3
  300.4 7.6 %slice-start = ((s8[6553600]{0:T(1024)(128)(4,1)}), s8[4194304]{0:T(1024)(128)(4,1)S(1)}, s32[]{:S(2)}) async-start(s8[6553600]{0:T(1024)(128)(4,1)} %bitcast.191), calls=%async_computation.8 | async-start | bytes 8388608 | tf_op jit(solution)/shard_map/while
  304.3 3.6 slice-start.1
  321.4 12.3 %copy-start = (f32[3072,2,128]{2,0,1:T(8,128)S(1)}, f32[3072,2,128]{2,0,1:T(8,128)}, u32[]{:S(2)}) copy-start(f32[3072,2,128]{2,0,1:T(8,128)} %get-tuple-element.235) | copy-start | bytes 9437188
  323.8 44.0 %all-to-all-start.6 = ((bf16[64,32,2,128]{3,2,1,0:T(2,128)(2,1)}), bf16[64,32,2,128]{3,2,1,0:T(2,128)(2,1)}, u32[]{:S(2)}, u32[]{:S(2)}) async-start(bf16[64,32,2,128]{3,2,1,0:T(2,128)(2,1)} %copy.117), calls=%async_computation.6 | async-start | bytes 2097152 | tf_op jit(solution)/shard_map/all_to_all | solution.py:167
  333.7 1.2 copy-start.10
  334.9 2.9 copy-start.6
  334.9 3.0 copy-start.20
  336.4 73.9 %collective-permute-start.1 = (f32[2,1024,2,128]{3,1,2,0:T(8,128)}, f32[2,1024,2,128]{3,1,2,0:T(8,128)}, u32[]{:S(2)}, u32[]{:S(2)}) collective-permute-start(f32[2,1024,2,128]{3,1,2,0:T(8,128)} %pad_maximum_fusion.13), channel_id=1, source_target_pairs={{4,0},{8,4},{12,8},{16,12},{20,16},{24,20},{28,24},{32,28},{36,32}... | collective-permute-start | bytes 6291464 | tf_op jit(solution)/shard_map/ppermute | solution.py:16
  338.7 2.0 copy-start.1
  367.8 30.6 %all-to-all-start.5 = ((bf16[64,32,2,128]{3,2,1,0:T(2,128)(2,1)}), bf16[64,32,2,128]{3,2,1,0:T(2,128)(2,1)}, u32[]{:S(2)}, u32[]{:S(2)}) async-start(bf16[64,32,2,128]{3,2,1,0:T(2,128)(2,1)} %copy.114), calls=%async_computation.5 | async-start | bytes 2097152 | tf_op jit(solution)/shard_map/all_to_all | solution.py:160
  379.8 364.3 %all-reduce.5.cloned.1.call-start = ((), (), s32[]{:S(2)}) async-start(), calls=%async_computation.7 | async-start | bytes 524288 | tf_op jit(solution)/shard_map/psum | solution.py:175
  379.8 3.3 copy-start.2
  388.0 3.9 copy-start.14
  388.0 4.8 copy-start.13
  398.4 2.5 copy-start.9
  398.4 2.5 copy-start.21
  410.2 3.1 copy-start.8
  427.6 2.2 copy-start.7
Sparse Core Ops, SparseCore 0:
  393.8 350.2 all-reduce.4
where the time goes:
time: 763 us; the launch traced here: 754 us
  waiting for transfers between devices  334 us (44%)
  local copies, waits for them, and re-layouts  176 us (23%)
  starting transfers between devices  90.7 us (12%)
  matrix products  78.5 us (10%)
  other arithmetic  57.4 us (8%)
  between operations  14.8 us (2%)
    psum x1, waiting for transfers between devices, body(): lax.psum((jnp.stack([pre_k_even, pre_k_odd], axis=2), jnp.stack([pre_v_ev...  298 us
    another operation x8, local copies, waits for them, and re-layouts, to_grid(): return array.reshape(rows_here, C, groups, DH)  29.7 us
    sub x5, matrix products, attend(): exp_terms = jnp.exp(scores - row_max)  29.7 us
    another operation x3, local copies, waits for them, and re-layouts, merge_heads(): jnp.stack([even_part, odd_part.reshape(length_here, groups, DH)], axis=2)  29.5 us
    all_to_all x1, starting transfers between devices, body(): lax.all_to_all(to_grid(q_odd), 'seq', split_axis=1, concat_axis=0, tiled=...  27 us
    unnamed x55, local copies, waits for them, and re-layouts  25.6 us
    all_to_all x1, waiting for transfers between devices, body(): lax.all_to_all(value_part[NPRE:].reshape(shape_out).astype(jnp.bfloat16),...  24.9 us
    convert_element_type x4, other arithmetic, attend(): attn_round = attn_probs.astype(jnp.bfloat16)  15.8 us
  transfers between devices with their start and end apart: 10, of which 5 were waited for; matrix products, arithmetic and copies ran while one was open for 39% of the time, Pallas kernels for 0%

commit v1 on v0

v1 whole, which is shorter than its diff:
```python
import math

import jax
import jax.numpy as jnp
from jax import lax
from jax.experimental import pallas as pl
from jax.experimental.pallas import tpu as pltpu
from jax.sharding import PartitionSpec as P

DH = 128
C = 1024
NPRE = 64
N = 32
W = C // N
QB = 256
KB = QB + C
SCALE = 1.0 / math.sqrt(DH)
LOG2E = SCALE * math.log2(math.e)
NEG = -1e30
MESH = pl.DeviceIdType.MESH
F32 = jnp.float32
BF16 = jnp.bfloat16

ORDER = [
    (0, 3, 2), (1, 0, 1), (0, 1, 3), (1, 2, 2), (0, 2, 1), (1, 3, 0), (0, 0, 3), (1, 1, 1),
    (1, 0, 0), (0, 2, 3), (1, 3, 2), (0, 1, 0), (1, 2, 1), (0, 3, 1), (1, 1, 3), (0, 0, 2),
    (1, 3, 3), (0, 2, 0), (1, 0, 2), (0, 1, 1), (1, 2, 3), (0, 3, 0), (1, 1, 0), (0, 2, 2),
    (1, 3, 1), (0, 0, 1), (1, 2, 0), (0, 1, 2), (1, 0, 3), (0, 3, 3), (1, 1, 2),
]


def nt(a, b):
    return lax.dot_general(a, b, (((1,), (1,)), ((), ())), preferred_element_type=F32)


def nn(a, b):
    return lax.dot_general(a, b, (((1,), (0,)), ((), ())), preferred_element_type=F32)


def tn(a, b):
    return lax.dot_general(a, b, (((0,), (0,)), ((), ())), preferred_element_type=F32)


def rows(x):
    return x.reshape(x.shape[-3] * W, DH) if x.ndim == 3 else x.reshape(-1, DH)


def softmax_parts(parts, dparts):
    top = parts[0].max(axis=0, keepdims=True)
    for s in parts[1:]:
        top = jnp.maximum(top, s.max(axis=0, keepdims=True))
    exps = [jnp.exp2((s - top) * LOG2E) for s in parts]
    total = sum(e.sum(axis=0, keepdims=True) for e in exps)
    mixed = sum((e * d).sum(axis=0, keepdims=True) for e, d in zip(exps, dparts))
    inv = 1.0 / total
    delta = mixed * inv
    probs = [e * inv for e in exps]
    ds = [p * (d - delta) for p, d in zip(probs, dparts)]
    return probs, ds


def kernel(
    q, k, v, g, pk, pv, dq_o, dk_o, dv_o, pkg_o, pvg_o,
    st, rc, qe, ge, kx, vx, pks, pvs, acck, accv, accp, oq, okk, ov, hs, hr,
    tin, tout, st2, rc2, pgs, prs, pag,
    lsem, ssem, rsem, hssem, hrsem, h2s, h2r, ssem2, rsem2, pss, prr, pas, par, osem,
):
    me = lax.axis_index("seq")
    z, x, y = me // 16, (me // 4) % 4, me % 4
    ids = [((z + dz) % 2) * 16 + ((x + dx) % 4) * 4 + (y + dy) % 4 for dz, dx, dy in ORDER]
    nxt = (me + 1) % N
    prv = (me + N - 1) % N

    def lane(hh):
        return pl.ds(hh * DH, DH)

    stage = []
    n = 0
    for h in range(2):
        for a, ref in enumerate((q, k, v, g)):
            for r in range(2):
                c = pltpu.make_async_copy(
                    ref.at[r, :, :, lane(2 * h + 1)], st.at[h, :, a, r], lsem.at[n]
                )
                c.start()
                stage.append(c)
                n += 1
    even = []
    for h in range(2):
        for ref, dst in ((k, kx), (v, vx), (q, qe), (g, ge)):
            off = 1 if ref is k or ref is v else 0
            for r in range(2):
                c = pltpu.make_async_copy(
                    ref.at[r, :, :, lane(2 * h)], dst.at[h, r + off], lsem.at[n]
                )
                c.start()
                even.append(c)
                n += 1

    bar = pltpu.get_barrier_semaphore()
    for i in ids:
        pl.semaphore_signal(bar, inc=1, device_id={"seq": i}, device_id_type=MESH)
    for hh in range(4):
        pks[hh] = pk[:, hh * DH : (hh + 1) * DH]
        pvs[hh] = pv[:, hh * DH : (hh + 1) * DH]
    acck[...] = jnp.zeros_like(acck)
    accv[...] = jnp.zeros_like(accv)
    accp[...] = jnp.zeros_like(accp)
    pl.semaphore_wait(bar, N - 1)

    def remote(src, dst, s, r, to):
        c = pltpu.make_async_remote_copy(
            src_ref=src, dst_ref=dst, send_sem=s, recv_sem=r,
            device_id={"seq": to}, device_id_type=MESH,
        )
        c.start()
        return c

    for c in even:
        c.wait()
    halo = []
    for h in range(2):
        for a, ref in enumerate((kx, vx)):
            halo.append(
                remote(ref.at[h, 2], ref.at[h, 0], hssem.at[2 * h + a], hrsem.at[2 * h + a], nxt)
            )
    for c in stage:
        c.wait()
    sent = [[], []]
    for h in range(2):
        for j, to in enumerate(ids):
            sent[h].append(
                remote(st.at[h, to], rc.at[h, me], ssem.at[h, j], rsem.at[h, j], to)
            )

    key_at = lax.broadcasted_iota(jnp.int32, (QB, QB), 0)
    query_at = lax.broadcasted_iota(jnp.int32, (QB, QB), 1)
    causal = key_at <= query_at

    def even_block(h, i):
        qb = rows(qe[h, i // 4, pl.ds((i % 4) * 8, 8)])
        gb = rows(ge[h, i // 4, pl.ds((i % 4) * 8, 8)])

        def window(ref, j):
            at = i + j
            return rows(ref[h, at // 4, pl.ds((at % 4) * 8, 8)])

        ks = [window(kx, j) for j in range(5)]
        vs = [window(vx, j) for j in range(5)]
        pkh, pvh = pks[2 * h], pvs[2 * h]
        s = [nt(kk, qb) for kk in ks]
        for j in range(4):
            s[j] = s[j] + jnp.where((me == 0) & (i + j < 4), NEG, 0.0).astype(F32)
        d = [nt(vv, gb) for vv in vs]
        s0 = jnp.where(causal, s[4], s[0])
        d0 = jnp.where(causal, d[4], d[0])
        probs, ds = softmax_parts(
            [nt(pkh, qb), s0, s[1], s[2], s[3]], [nt(pvh, gb), d0, d[1], d[2], d[3]]
        )

        def spread(parts):
            pre, edge, mid = parts[0], parts[1], parts[2:]
            zero = jnp.zeros_like(edge)
            out = [jnp.where(causal, zero, edge), *mid, jnp.where(causal, edge, zero)]
            return pre.astype(BF16), [o.astype(BF16) for o in out]

        p_pre, p = spread(probs)
        ds_pre, dd = spread(ds)
        dq = tn(pkh, ds_pre)
        for j in range(5):
            at = pl.ds((i + j) * QB, QB)
            accv[h, at] += nn(p[j], gb)
            acck[h, at] += nn(dd[j], qb)
            dq = dq + tn(ks[j], dd[j])
        accp[0, 2 * h] += nn(ds_pre, qb)
        accp[1, 2 * h] += nn(p_pre, gb)
        oq[h, i // 4, pl.ds((i % 4) * 8, 8)] = (
            (jnp.transpose(dq) * SCALE).astype(BF16).reshape(QB // W, W, DH)
        )

    @pl.loop(0, 8)
    def _(step):
        even_block(step // 4, step % 4 + 4)

    for c in halo:
        c.wait_recv()

    @pl.loop(0, 8)
    def _(step):
        even_block(step // 4, step % 4)

    back = []
    for h in range(2):
        hs[h, 0] = (acck[h, :C] * SCALE).astype(BF16)
        hs[h, 1] = accv[h, :C].astype(BF16)
        back.append(remote(hs.at[h], hr.at[h], h2s.at[h], h2r.at[h], prv))

    key_col = key_at // 64
    query_col = query_at // 64
    column = (key_col == query_col) & (key_at % 64 <= query_at % 64)

    def odd_head(h):
        for a in range(4):
            @pl.loop(0, N)
            def _(b):
                tin[a, pl.ds(b * 64, 64)] = rows(rc[h, b, a]).astype(F32)

        pkh, pvh = pks[2 * h + 1], pvs[2 * h + 1]

        @pl.loop(0, W // 4)
        def _(cg):
            def take(a):
                return jnp.concatenate(
                    [tin[a, pl.ds(cg * 4 + cc, 64, stride=W), :] for cc in range(4)], axis=0
                ).astype(BF16)

            qb, kb, vb, gb = take(0), take(1), take(2), take(3)
            s = jnp.where(column, nt(kb, qb), NEG)
            probs, ds = softmax_parts([nt(pkh, qb), s], [nt(pvh, gb), nt(vb, gb)])
            p_pre, p = probs[0].astype(BF16), probs[1].astype(BF16)
            ds_pre, dd = ds[0].astype(BF16), ds[1].astype(BF16)
            dq = jnp.transpose(tn(pkh, ds_pre) + tn(kb, dd)) * SCALE
            dk = nn(dd, qb) * SCALE
            dv = nn(p, gb)
            accp[0, 2 * h + 1] += nn(ds_pre, qb)
            accp[1, 2 * h + 1] += nn(p_pre, gb)
            for a, val in enumerate((dq, dk, dv)):
                for cc in range(4):
                    tout[a, pl.ds(cg * 4 + cc, 64, stride=W), :] = val[cc * 64 : cc * 64 + 64]

        for a in range(3):
            @pl.loop(0, N)
            def _(b):
                st2[h, b, a] = tout[a, pl.ds(b * 64, 64)].astype(BF16).reshape(2, W, DH)

    sent2 = [[], []]
    own = []

    def send_back(h):
        own.append(pltpu.make_async_copy(st2.at[h, me], rc2.at[h, me], osem.at[h]))
        own[-1].start()
        for j, to in enumerate(ids):
            sent2[h].append(
                remote(st2.at[h, to], rc2.at[h, me], ssem2.at[h, j], rsem2.at[h, j], to)
            )

    for h in range(2):
        mine = pltpu.make_async_copy(st.at[h, me], rc.at[h, me], osem.at[2 + h])
        mine.start()
        mine.wait()
        for c in sent[h]:
            c.wait_recv()
        odd_head(h)
        if h == 0:
            send_back(0)

    for a in range(2):
        for hh in range(4):
            part = accp[a, hh] * SCALE if a == 0 else accp[a, hh]
            at = (a * 4 + hh) * 4
            pgs[at : at + 4] = part.astype(BF16).reshape(4, 16, DH)
    scat = []
    for j, to in enumerate(ids):
        scat.append(remote(pgs.at[to], prs.at[me], pss.at[j], prr.at[j], to))
    send_back(1)
    prs[me] = pgs[me]
    for c in scat:
        c.wait_recv()
    tot = prs[0].astype(F32)
    for j in range(1, N):
        tot = tot + prs[j].astype(F32)
    pag[me] = tot
    gath = []
    for j, to in enumerate(ids):
        gath.append(remote(pag.at[me], pag.at[me], pas.at[j], par.at[j], to))

    n_out = 4
    outs = []

    def put(src, dst, at):
        c = pltpu.make_async_copy(src, dst, osem.at[at])
        c.start()
        outs.append(c)

    for h in range(2):
        back[h].wait_recv()
        for a, (acc, o) in enumerate(((acck, okk), (accv, ov))):
            f = SCALE if a == 0 else 1.0
            o[h, 0] = (acc[h, C : 2 * C] * f).astype(BF16).reshape(N, W, DH)
            o[h, 1] = (acc[h, 2 * C :] * f + hr[h, a].astype(F32)).astype(BF16).reshape(N, W, DH)
        for o, dst in ((oq, dq_o), (okk, dk_o), (ov, dv_o)):
            put(o.at[h], dst.at[:, :, :, lane(2 * h)], n_out)
            n_out += 1

    for h in range(2):
        own[h].wait()
        for c in sent2[h]:
            c.wait_recv()
        for a, dst in enumerate((dq_o, dk_o, dv_o)):
            for r in range(2):
                put(rc2.at[h, :, a, r], dst.at[r, :, :, lane(2 * h + 1)], n_out)
                n_out += 1

    for c in gath:
        c.wait_recv()
    for a, dst in enumerate((pkg_o, pvg_o)):
        for hh in range(4):
            at = (a * 4 + hh) * 4
            dst[:, hh * DH : (hh + 1) * DH] = pag[at : at + 4].reshape(NPRE, DH)

    for c in outs:
        c.wait()
    for c in halo + sent[0] + sent[1] + back + sent2[0] + sent2[1] + scat + gath:
        c.wait_send()


def body(queries, key_field, value_field, out_grad, prefix_keys, prefix_values):
    grid = (2, N, W, 4 * DH)
    anyspace = pl.BlockSpec(memory_space=pl.ANY)
    vm = pl.BlockSpec(memory_space=pltpu.VMEM)
    dma = pltpu.SemaphoreType.DMA
    big = jax.ShapeDtypeStruct(grid, BF16)
    pre = jax.ShapeDtypeStruct((NPRE, 4 * DH), F32)
    dq, dk, dv, pkg, pvg = pl.pallas_call(
        kernel,
        name="strided_backward",
        out_shape=(big, big, big, pre, pre),
        in_specs=[anyspace] * 4 + [vm] * 2,
        out_specs=[anyspace] * 3 + [vm] * 2,
        scratch_shapes=[
            pltpu.VMEM((2, N, 4, 2, W, DH), BF16),
            pltpu.VMEM((2, N, 4, 2, W, DH), BF16),
            pltpu.VMEM((2, 2, N, W, DH), BF16),
            pltpu.VMEM((2, 2, N, W, DH), BF16),
            pltpu.VMEM((2, 3, N, W, DH), BF16),
            pltpu.VMEM((2, 3, N, W, DH), BF16),
            pltpu.VMEM((4, NPRE, DH), BF16),
            pltpu.VMEM((4, NPRE, DH), BF16),
            pltpu.VMEM((2, 3 * C, DH), F32),
            pltpu.VMEM((2, 3 * C, DH), F32),
            pltpu.VMEM((2, 4, NPRE, DH), F32),
            pltpu.VMEM((2, 2, N, W, DH), BF16),
            pltpu.VMEM((2, 2, N, W, DH), BF16),
            pltpu.VMEM((2, 2, N, W, DH), BF16),
            pltpu.VMEM((2, 2, C, DH), BF16),
            pltpu.VMEM((2, 2, C, DH), BF16),
            pltpu.VMEM((4, 2 * C, DH), F32),
            pltpu.VMEM((3, 2 * C, DH), F32),
            pltpu.VMEM((2, N, 3, 2, W, DH), BF16),
            pltpu.VMEM((2, N, 3, 2, W, DH), BF16),
            pltpu.VMEM((N, 16, DH), BF16),
            pltpu.VMEM((N, 16, DH), BF16),
            pltpu.VMEM((N, 16, DH), F32),
            dma((32,)),
            dma((2, N - 1)), dma((2, N - 1)),
            dma((4,)), dma((4,)), dma((2,)), dma((2,)),
            dma((2, N - 1)), dma((2, N - 1)),
            dma((N - 1,)), dma((N - 1,)), dma((N - 1,)), dma((N - 1,)),
            dma((22,)),
        ],
        compiler_params=pltpu.CompilerParams(
            collective_id=0, has_side_effects=True, vmem_limit_bytes=60 << 20
        ),
    )(
        *[a.reshape(grid) for a in (queries, key_field, value_field, out_grad)],
        prefix_keys,
        prefix_values,
    )
    flat = (2 * C, 4 * DH)
    return dq.reshape(flat), dk.reshape(flat), dv.reshape(flat), pkg, pvg


def solution(mesh):
    split = P("seq", "head")
    shared = P(None, "head")
    return jax.shard_map(
        body,
        mesh=mesh,
        in_specs=(split, split, split, split, shared, shared),
        out_specs=(split, split, split, shared, shared),
        check_vma=False,
    )
```

time: 763 us -> 170 us (0.22)
  waiting for transfers between devices: 334 us -> 0 us
  local copies, waits for them, and re-layouts: 176 us -> 8.18 us
  Pallas kernels: 0 us -> 160 us
  starting transfers between devices: 90.7 us -> 0 us
  matrix products: 78.5 us -> 0 us
  other arithmetic: 57.4 us -> 0 us
  between operations: 14.8 us -> 0.65 us
    psum x1 -> x0, waiting for transfers between devices: 298 us -> none  [body(): lax.psum((jnp.stack([pre_k_even, pre_k_odd], axis=2), jnp.stack([pre_v_ev...]
    pallas_call x0 -> x1, Pallas kernels: none -> 160 us  [body(): pl.pallas_call(kernel, name='strided_backward', out_shape=(big, big, big,...]
    all_to_all x7 -> x0, starting transfers between devices: 84.6 us -> none  [the longest x1 27 us: body(): lax.all_to_all(to_grid(q_odd), 'seq', split_axis=1, concat_axis=0, tiled=...]
    another operation x16 -> x0, local copies, waits for them, and re-layouts: 63.1 us -> none  [the longest x8 29.7 us: to_grid(): return array.reshape(rows_here, C, groups, DH)]
    dot_general x25 -> x0, matrix products: 48.9 us -> none  [the longest x5 13.4 us: attend(): jnp.einsum('bqm,mbd->qbd', attn_round, value_all, preferred_element_type=...]
    all_to_all x7 -> x0, waiting for transfers between devices: 36.2 us -> none  [the longest x1 24.9 us: body(): lax.all_to_all(value_part[NPRE:].reshape(shape_out).astype(jnp.bfloat16),...]
    sub x5 -> x0, matrix products: 29.7 us -> none  [attend(): exp_terms = jnp.exp(scores - row_max)]
    dynamic_slice x28 -> x0, local copies, waits for them, and re-layouts: 22.3 us -> none  [the longest x8 7.44 us: row_step(): grad_blk = lax.dynamic_slice_in_dim(g_even, blk_start, q_blk, 0)]
  transfers between devices with their start and end apart: 10 -> 0, of which waited for: 5 -> 0; matrix products, arithmetic and copies ran while one was open for 39% -> 0% of each run, Pallas kernels for 0% -> 0%
where the time goes in v1:
time: 170 us; the launch traced here: 169 us
  Pallas kernels  160 us (94%)
  local copies, waits for them, and re-layouts  8.18 us (5%)
    pallas_call x1, Pallas kernels, body(): pl.pallas_call(kernel, name='strided_backward', out_shape=(big, big, big,...  160 us
    unnamed x13, local copies, waits for them, and re-layouts  8.18 us

profile of v1, /device:TPU:0, one launch (start us, length us, event | category | flops | bytes accessed | tf_op | source)
XLA Modules:
  0.0 168.8 jit_solution(5238790427939345434)
XLA Ops:
  0.6 160.0 %strided_backward.1 = (bf16[2,32,32,512]{3,2,1,0:T(8,128)(2,1)}, bf16[2,32,32,512]{3,2,1,0:T(8,128)(2,1)}, bf16[2,32,32,512]{3,2,1,0:T(8,128)(2,1)}, f32[64,512]{1,0:T(8,128)}, f32[64,512]{1,0:T(8,128)}) custom-call(bf16[2,32,32,512]{3,2,1,0:T(8,128)(2,1)} %bitcast.10, bf16[2,32,32,512]{3,2,1,0:T(8,128)(2,1)} %bitcast.11, bf16[2,32,32,512]{3,2,1,0:T(8,128)(2,1)} %bitcast.12, ...), custom_call_target="tpu_custom_call" | custom-call | tf_op jit(solution)/shard_map/strided_backward/pallas_call | solution.py:324
  160.6 0.0 copy-start.1
  160.7 3.2 %copy.16 = bf16[2048,512]{1,0:T(8,128)(2,1)} copy(bf16[2048,512]{1,0:T(8,128)(2,1)} %bitcast.9) | data formatting | bytes 4194304
  163.9 0.0 copy-done.1
  163.9 0.0 copy-start
  163.9 1.3 copy.17
  165.2 1.0 copy-done
  166.2 0.0 copy-start.3
  166.2 0.0 copy-start.2
  166.2 1.3 copy.18
  167.5 0.0 copy-done.3
  167.5 0.7 copy.19
  168.2 0.0 copy-done.2
  168.2 0.7 copy.20
Async XLA Ops:
  160.6 3.2 %copy-start.1 = (bf16[2,32,32,512]{3,2,1,0:T(8,128)(2,1)S(1)}, bf16[2,32,32,512]{3,2,1,0:T(8,128)(2,1)}, u32[]{:S(2)}) copy-start(bf16[2,32,32,512]{3,2,1,0:T(8,128)(2,1)} %get-tuple-element.11) | copy-start | bytes 6291460
  163.9 2.3 %copy-start = (bf16[2,32,32,512]{3,2,1,0:T(8,128)(2,1)S(1)}, bf16[2,32,32,512]{3,2,1,0:T(8,128)(2,1)}, u32[]{:S(2)}) copy-start(bf16[2,32,32,512]{3,2,1,0:T(8,128)(2,1)} %get-tuple-element.12) | copy-start | bytes 6291460
  166.2 1.3 copy-start.3
  166.2 2.0 %copy-start.2 = (f32[64,512]{1,0:T(8,128)S(1)}, f32[64,512]{1,0:T(8,128)}, u32[]{:S(2)}) copy-start(f32[64,512]{1,0:T(8,128)} %get-tuple-element.24) | copy-start | bytes 393220

commit v2 on v1

--- a/solution.py
+++ b/solution.py
@@ -22,10 +22,10 @@
 BF16 = jnp.bfloat16
 
 ORDER = [
-    (0, 3, 2), (1, 0, 1), (0, 1, 3), (1, 2, 2), (0, 2, 1), (1, 3, 0), (0, 0, 3), (1, 1, 1),
-    (1, 0, 0), (0, 2, 3), (1, 3, 2), (0, 1, 0), (1, 2, 1), (0, 3, 1), (1, 1, 3), (0, 0, 2),
-    (1, 3, 3), (0, 2, 0), (1, 0, 2), (0, 1, 1), (1, 2, 3), (0, 3, 0), (1, 1, 0), (0, 2, 2),
-    (1, 3, 1), (0, 0, 1), (1, 2, 0), (0, 1, 2), (1, 0, 3), (0, 3, 3), (1, 1, 2),
+    (1, 2, 3), (0, 0, 1), (1, 3, 2), (0, 1, 0), (1, 2, 1), (0, 0, 3), (1, 2, 2), (0, 3, 0),
+    (1, 1, 2), (0, 2, 0), (1, 0, 2), (0, 1, 1), (1, 3, 3), (0, 0, 2), (1, 2, 0), (0, 3, 3),
+    (1, 1, 1), (1, 0, 0), (0, 2, 2), (0, 3, 1), (1, 1, 3), (0, 1, 2), (1, 3, 0), (0, 1, 3),
+    (1, 3, 1), (0, 2, 3), (1, 0, 1), (1, 0, 3), (0, 2, 1), (1, 1, 0), (0, 3, 2),
 ]
 
 
@@ -54,15 +54,16 @@
     mixed = sum((e * d).sum(axis=0, keepdims=True) for e, d in zip(exps, dparts))
     inv = 1.0 / total
     delta = mixed * inv
+    lse = top * LOG2E + jnp.log2(total)
     probs = [e * inv for e in exps]
     ds = [p * (d - delta) for p, d in zip(probs, dparts)]
-    return probs, ds
+    return probs, ds, lse, delta
 
 
 def kernel(
-    q, k, v, g, pk, pv, dq_o, dk_o, dv_o, pkg_o, pvg_o,
-    st, rc, qe, ge, kx, vx, pks, pvs, acck, accv, accp, oq, okk, ov, hs, hr,
-    tin, tout, st2, rc2, pgs, prs, pag,
+    q, k, v, g, pk, pv, ev, rc2, pag,
+    st, rc, qe, ge, kx, vx, qn, gn, pks, pvs, acck, accv, accp, oe, stat, statn,
+    tin, tout, st2, pgs, prs, psum,
     lsem, ssem, rsem, hssem, hrsem, h2s, h2r, ssem2, rsem2, pss, prr, pas, par, osem,
 ):
     me = lax.axis_index("seq")
@@ -119,19 +120,30 @@
     for c in even:
         c.wait()
     halo = []
-    for h in range(2):
-        for a, ref in enumerate((kx, vx)):
-            halo.append(
-                remote(ref.at[h, 2], ref.at[h, 0], hssem.at[2 * h + a], hrsem.at[2 * h + a], nxt)
-            )
-    for c in stage:
-        c.wait()
+
+    def send_halo(n):
+        m = n // 2
+        h, a, p = m // 8, (m // 4) % 2, m % 4
+        part = pl.ds(p * 8, 8)
+        if n % 2 == 0:
+            ref = (kx, vx)[a]
+            src, dst, to = ref.at[h, 2, part], ref.at[h, 0, part], nxt
+        else:
+            src, dst, to = (qe, ge)[a].at[h, 0, part], (qn, gn)[a].at[h, part], prv
+        halo.append(remote(src, dst, hssem.at[n], hrsem.at[n], to))
+
     sent = [[], []]
     for h in range(2):
+        for c in stage[8 * h : 8 * h + 8]:
+            c.wait()
         for j, to in enumerate(ids):
+            if h == 0:
+                send_halo(j)
             sent[h].append(
                 remote(st.at[h, to], rc.at[h, me], ssem.at[h, j], rsem.at[h, j], to)
             )
+        if h == 0:
+            send_halo(31)
 
     key_at = lax.broadcasted_iota(jnp.int32, (QB, QB), 0)
     query_at = lax.broadcasted_iota(jnp.int32, (QB, QB), 1)
@@ -154,7 +166,7 @@
         d = [nt(vv, gb) for vv in vs]
         s0 = jnp.where(causal, s[4], s[0])
         d0 = jnp.where(causal, d[4], d[0])
-        probs, ds = softmax_parts(
+        probs, ds, lse, delta = softmax_parts(
             [nt(pkh, qb), s0, s[1], s[2], s[3]], [nt(pvh, gb), d0, d[1], d[2], d[3]]
         )
 
@@ -174,40 +186,61 @@
             dq = dq + tn(ks[j], dd[j])
         accp[0, 2 * h] += nn(ds_pre, qb)
         accp[1, 2 * h] += nn(p_pre, gb)
-        oq[h, i // 4, pl.ds((i % 4) * 8, 8)] = (
+        oe[h, 0, i // 4, pl.ds((i % 4) * 8, 8)] = (
             (jnp.transpose(dq) * SCALE).astype(BF16).reshape(QB // W, W, DH)
         )
+        return lse, delta
 
     @pl.loop(0, 8)
     def _(step):
         even_block(step // 4, step % 4 + 4)
 
-    for c in halo:
-        c.wait_recv()
-
-    @pl.loop(0, 8)
-    def _(step):
-        even_block(step // 4, step % 4)
-
-    back = []
-    for h in range(2):
-        hs[h, 0] = (acck[h, :C] * SCALE).astype(BF16)
-        hs[h, 1] = accv[h, :C].astype(BF16)
-        back.append(remote(hs.at[h], hr.at[h], h2s.at[h], h2r.at[h], prv))
+    def first_row():
+        for c in halo:
+            c.wait_recv()
+
+        @pl.loop(0, 8)
+        def _(step):
+            lse, delta = even_block(step // 4, step % 4)
+            stat[0, pl.ds(step, 1)] = lse
+            stat[1, pl.ds(step, 1)] = delta
+
+        return remote(stat, statn, h2s.at[0], h2r.at[0], prv)
+
+    def next_row():
+        off = jnp.where(me == N - 1, -NEG, 0.0).astype(F32)
+
+        @pl.loop(0, 4)
+        def _(j):
+            @pl.loop(0, j + 1)
+            def _(i):
+                for h in range(2):
+                    kb = rows(kx[h, 2, pl.ds(j * 8, 8)])
+                    vb = rows(vx[h, 2, pl.ds(j * 8, 8)])
+                    qb = rows(qn[h, pl.ds(i * 8, 8)])
+                    gb = rows(gn[h, pl.ds(i * 8, 8)])
+                    lse = statn[0, pl.ds(h * 4 + i, 1)] + off
+                    delta = statn[1, pl.ds(h * 4 + i, 1)]
+                    s = jnp.where(causal & (i == j), NEG, nt(kb, qb))
+                    p = jnp.exp2(s * LOG2E - lse)
+                    ds = p * (nt(vb, gb) - delta)
+                    at = pl.ds(2 * C + j * QB, QB)
+                    accv[h, at] += nn(p.astype(BF16), gb)
+                    acck[h, at] += nn(ds.astype(BF16), qb)
 
     key_col = key_at // 64
     query_col = query_at // 64
     column = (key_col == query_col) & (key_at % 64 <= query_at % 64)
 
     def odd_head(h):
-        for a in range(4):
-            @pl.loop(0, N)
-            def _(b):
+        @pl.loop(0, N, unroll=2)
+        def _(b):
+            for a in range(4):
                 tin[a, pl.ds(b * 64, 64)] = rows(rc[h, b, a]).astype(F32)
 
         pkh, pvh = pks[2 * h + 1], pvs[2 * h + 1]
 
-        @pl.loop(0, W // 4)
+        @pl.loop(0, W // 4, unroll=2)
         def _(cg):
             def take(a):
                 return jnp.concatenate(
@@ -216,7 +249,7 @@
 
             qb, kb, vb, gb = take(0), take(1), take(2), take(3)
             s = jnp.where(column, nt(kb, qb), NEG)
-            probs, ds = softmax_parts([nt(pkh, qb), s], [nt(pvh, gb), nt(vb, gb)])
+            probs, ds, _, _ = softmax_parts([nt(pkh, qb), s], [nt(pvh, gb), nt(vb, gb)])
             p_pre, p = probs[0].astype(BF16), probs[1].astype(BF16)
             ds_pre, dd = ds[0].astype(BF16), ds[1].astype(BF16)
             dq = jnp.transpose(tn(pkh, ds_pre) + tn(kb, dd)) * SCALE
@@ -228,31 +261,36 @@
                 for cc in range(4):
                     tout[a, pl.ds(cg * 4 + cc, 64, stride=W), :] = val[cc * 64 : cc * 64 + 64]
 
-        for a in range(3):
-            @pl.loop(0, N)
-            def _(b):
+        @pl.loop(0, N, unroll=2)
+        def _(b):
+            for a in range(3):
                 st2[h, b, a] = tout[a, pl.ds(b * 64, 64)].astype(BF16).reshape(2, W, DH)
 
     sent2 = [[], []]
-    own = []
-
-    def send_back(h):
-        own.append(pltpu.make_async_copy(st2.at[h, me], rc2.at[h, me], osem.at[h]))
-        own[-1].start()
-        for j, to in enumerate(ids):
+    outs = []
+
+    def put(src, dst):
+        c = pltpu.make_async_copy(src, dst, osem.at[len(outs)])
+        c.start()
+        outs.append(c)
+
+    def send_back(h, lo, hi):
+        for j in range(lo, hi):
             sent2[h].append(
-                remote(st2.at[h, to], rc2.at[h, me], ssem2.at[h, j], rsem2.at[h, j], to)
+                remote(st2.at[h, ids[j]], rc2.at[h, me], ssem2.at[h, j], rsem2.at[h, j], ids[j])
             )
 
     for h in range(2):
-        mine = pltpu.make_async_copy(st.at[h, me], rc.at[h, me], osem.at[2 + h])
+        mine = pltpu.make_async_copy(st.at[h, me], rc.at[h, me], lsem.at[32 + h])
         mine.start()
         mine.wait()
         for c in sent[h]:
             c.wait_recv()
         odd_head(h)
+        put(st2.at[h, me], rc2.at[h, me])
         if h == 0:
-            send_back(0)
+            send_back(0, 0, N - 1)
+            stats = first_row()
 
     for a in range(2):
         for hh in range(4):
@@ -262,56 +300,50 @@
     scat = []
     for j, to in enumerate(ids):
         scat.append(remote(pgs.at[to], prs.at[me], pss.at[j], prr.at[j], to))
-    send_back(1)
+    send_back(1, 0, 4)
     prs[me] = pgs[me]
     for c in scat:
         c.wait_recv()
     tot = prs[0].astype(F32)
     for j in range(1, N):
         tot = tot + prs[j].astype(F32)
-    pag[me] = tot
+    psum[...] = tot.astype(BF16)
+    put(psum, pag.at[me])
     gath = []
     for j, to in enumerate(ids):
-        gath.append(remote(pag.at[me], pag.at[me], pas.at[j], par.at[j], to))
-
-    n_out = 4
-    outs = []
-
-    def put(src, dst, at):
-        c = pltpu.make_async_copy(src, dst, osem.at[at])
-        c.start()
-        outs.append(c)
-
-    for h in range(2):
-        back[h].wait_recv()
-        for a, (acc, o) in enumerate(((acck, okk), (accv, ov))):
-            f = SCALE if a == 0 else 1.0
-            o[h, 0] = (acc[h, C : 2 * C] * f).astype(BF16).reshape(N, W, DH)
-            o[h, 1] = (acc[h, 2 * C :] * f + hr[h, a].astype(F32)).astype(BF16).reshape(N, W, DH)
-        for o, dst in ((oq, dq_o), (okk, dk_o), (ov, dv_o)):
-            put(o.at[h], dst.at[:, :, :, lane(2 * h)], n_out)
-            n_out += 1
-
-    for h in range(2):
-        own[h].wait()
+        gath.append(remote(psum, pag.at[me], pas.at[j], par.at[j], to))
+    send_back(1, 4, N - 1)
+
+    stats.wait_recv()
+    next_row()
+    for h in range(2):
+        for a, acc in ((1, acck), (2, accv)):
+            for r in range(2):
+                part = acc[h, (1 + r) * C : (2 + r) * C]
+                part = part * SCALE if a == 1 else part
+                oe[h, a, r] = part.astype(BF16).reshape(N, W, DH)
+        put(oe.at[h], ev.at[h])
+
+    for h in range(2):
         for c in sent2[h]:
             c.wait_recv()
-        for a, dst in enumerate((dq_o, dk_o, dv_o)):
-            for r in range(2):
-                put(rc2.at[h, :, a, r], dst.at[r, :, :, lane(2 * h + 1)], n_out)
-                n_out += 1
-
     for c in gath:
         c.wait_recv()
-    for a, dst in enumerate((pkg_o, pvg_o)):
+    for c in outs:
+        c.wait()
+    for c in halo + sent[0] + sent[1] + [stats] + sent2[0] + sent2[1] + scat + gath:
+        c.wait_send()
+
+
+def merge(ev, od, pag, dq, dk, dv, pkg, pvg):
+    for a, out in enumerate((dq, dk, dv)):
+        for h in range(2):
+            out[:, 2 * h * DH : (2 * h + 1) * DH] = ev[h, a, 0].reshape(-1, DH)
+            out[:, (2 * h + 1) * DH : (2 * h + 2) * DH] = od[h, :, a, 0].reshape(-1, DH)
+    for a, out in enumerate((pkg, pvg)):
         for hh in range(4):
             at = (a * 4 + hh) * 4
-            dst[:, hh * DH : (hh + 1) * DH] = pag[at : at + 4].reshape(NPRE, DH)
-
-    for c in outs:
-        c.wait()
-    for c in halo + sent[0] + sent[1] + back + sent2[0] + sent2[1] + scat + gath:
-        c.wait_send()
+            out[:, hh * DH : (hh + 1) * DH] = pag[at : at + 4].reshape(NPRE, DH).astype(F32)
 
 
 def body(queries, key_field, value_field, out_grad, prefix_keys, prefix_values):
@@ -319,14 +351,16 @@
     anyspace = pl.BlockSpec(memory_space=pl.ANY)
     vm = pl.BlockSpec(memory_space=pltpu.VMEM)
     dma = pltpu.SemaphoreType.DMA
-    big = jax.ShapeDtypeStruct(grid, BF16)
-    pre = jax.ShapeDtypeStruct((NPRE, 4 * DH), F32)
-    dq, dk, dv, pkg, pvg = pl.pallas_call(
+    ev, od, pag = pl.pallas_call(
         kernel,
         name="strided_backward",
-        out_shape=(big, big, big, pre, pre),
+        out_shape=(
+            jax.ShapeDtypeStruct((2, 3, 2, N, W, DH), BF16),
+            jax.ShapeDtypeStruct((2, N, 3, 2, W, DH), BF16),
+            jax.ShapeDtypeStruct((N, 16, DH), BF16),
+        ),
         in_specs=[anyspace] * 4 + [vm] * 2,
-        out_specs=[anyspace] * 3 + [vm] * 2,
+        out_specs=[anyspace] * 3,
         scratch_shapes=[
             pltpu.VMEM((2, N, 4, 2, W, DH), BF16),
             pltpu.VMEM((2, N, 4, 2, W, DH), BF16),
@@ -334,29 +368,28 @@
             pltpu.VMEM((2, 2, N, W, DH), BF16),
             pltpu.VMEM((2, 3, N, W, DH), BF16),
             pltpu.VMEM((2, 3, N, W, DH), BF16),
+            pltpu.VMEM((2, N, W, DH), BF16),
+            pltpu.VMEM((2, N, W, DH), BF16),
             pltpu.VMEM((4, NPRE, DH), BF16),
             pltpu.VMEM((4, NPRE, DH), BF16),
             pltpu.VMEM((2, 3 * C, DH), F32),
             pltpu.VMEM((2, 3 * C, DH), F32),
             pltpu.VMEM((2, 4, NPRE, DH), F32),
-            pltpu.VMEM((2, 2, N, W, DH), BF16),
-            pltpu.VMEM((2, 2, N, W, DH), BF16),
-            pltpu.VMEM((2, 2, N, W, DH), BF16),
-            pltpu.VMEM((2, 2, C, DH), BF16),
-            pltpu.VMEM((2, 2, C, DH), BF16),
+            pltpu.VMEM((2, 3, 2, N, W, DH), BF16),
+            pltpu.VMEM((2, 8, QB), F32),
+            pltpu.VMEM((2, 8, QB), F32),
             pltpu.VMEM((4, 2 * C, DH), F32),
             pltpu.VMEM((3, 2 * C, DH), F32),
             pltpu.VMEM((2, N, 3, 2, W, DH), BF16),
-            pltpu.VMEM((2, N, 3, 2, W, DH), BF16),
             pltpu.VMEM((N, 16, DH), BF16),
             pltpu.VMEM((N, 16, DH), BF16),
-            pltpu.VMEM((N, 16, DH), F32),
-            dma((32,)),
+            pltpu.VMEM((16, DH), BF16),
+            dma((34,)),
             dma((2, N - 1)), dma((2, N - 1)),
-            dma((4,)), dma((4,)), dma((2,)), dma((2,)),
+            dma((32,)), dma((32,)), dma((1,)), dma((1,)),
             dma((2, N - 1)), dma((2, N - 1)),
             dma((N - 1,)), dma((N - 1,)), dma((N - 1,)), dma((N - 1,)),
-            dma((22,)),
+            dma((5,)),
         ],
         compiler_params=pltpu.CompilerParams(
             collective_id=0, has_side_effects=True, vmem_limit_bytes=60 << 20
@@ -366,8 +399,26 @@
         prefix_keys,
         prefix_values,
     )
-    flat = (2 * C, 4 * DH)
-    return dq.reshape(flat), dk.reshape(flat), dv.reshape(flat), pkg, pvg
+    steps = 8
+    wide = pl.BlockSpec((2 * C // steps, 4 * DH), lambda p: (p, 0))
+    pre = pl.BlockSpec((NPRE, 4 * DH), lambda p: (0, 0))
+    big = jax.ShapeDtypeStruct((2 * C, 4 * DH), BF16)
+    small = jax.ShapeDtypeStruct((NPRE, 4 * DH), F32)
+    blk = 2 * N // steps
+    half = steps // 2
+    return pl.pallas_call(
+        merge,
+        name="merge_heads",
+        grid=(steps,),
+        out_shape=(big, big, big, small, small),
+        in_specs=[
+            pl.BlockSpec((2, 3, 1, blk, W, DH), lambda p: (0, 0, p // half, p % half, 0, 0)),
+            pl.BlockSpec((2, blk, 3, 1, W, DH), lambda p: (0, p % half, 0, p // half, 0, 0)),
+            pl.BlockSpec((N, 16, DH), lambda p: (0, 0, 0)),
+        ],
+        out_specs=[wide] * 3 + [pre] * 2,
+        compiler_params=pltpu.CompilerParams(vmem_limit_bytes=60 << 20),
+    )(ev, od, pag)
 
 
 def solution(mesh):

time: 170 us -> 149 us (0.88)
  Pallas kernels: 160 us -> 148 us
  local copies, waits for them, and re-layouts: 8.18 us -> 0 us
    pallas_call x1 -> x2, Pallas kernels: 160 us -> 148 us  [the longest x1 140 us: body(): pl.pallas_call(kernel, name='strided_backward', out_shape=(jax.ShapeDtype...]
    unnamed x13 -> x0, local copies, waits for them, and re-layouts: 8.18 us -> none
where the time goes in v2:
time: 149 us
  Pallas kernels  148 us (99%)
    pallas_call x1, Pallas kernels, body(): pl.pallas_call(kernel, name='strided_backward', out_shape=(jax.ShapeDtype...  140 us
    pallas_call x1, Pallas kernels, body(): pl.pallas_call(merge, name='merge_heads', grid=(steps,), out_shape=(big,...  8.2 us

profile of v2, /device:TPU:0, one launch (start us, length us, event | category | flops | bytes accessed | tf_op | source)
XLA Modules:
  0.0 149.0 jit_solution(1806625187250514672)
XLA Ops:
  0.6 140.2 %strided_backward.1 = (bf16[2,3,2,32,32,128]{5,4,3,2,1,0:T(8,128)(2,1)}, bf16[2,32,3,2,32,128]{5,4,3,2,1,0:T(8,128)(2,1)}, bf16[32,16,128]{2,1,0:T(8,128)(2,1)}) custom-call(bf16[2,32,32,512]{3,2,1,0:T(8,128)(2,1)} %bitcast.4, bf16[2,32,32,512]{3,2,1,0:T(8,128)(2,1)} %bitcast.5, bf16[2,32,32,512]{3,2,1,0:T(8,128)(2,1)} %bitcast.6, ...), custom_call_target="tpu_custom_call" | custom-call | tf_op jit(solution)/shard_map/strided_backward/pallas_call | solution.py:354
  140.8 8.2 %merge_heads.1 = (bf16[2048,512]{1,0:T(8,128)(2,1)}, bf16[2048,512]{1,0:T(8,128)(2,1)}, bf16[2048,512]{1,0:T(8,128)(2,1)}, f32[64,512]{1,0:T(8,128)}, f32[64,512]{1,0:T(8,128)}) custom-call(bf16[2,3,2,32,32,128]{5,4,3,2,1,0:T(8,128)(2,1)} %get-tuple-element.8.ev, bf16[2,32,3,2,32,128]{5,4,3,2,1,0:T(8,128)(2,1)} %get-tuple-element.9.od, ...), custom_call_target="tpu_custom_call" | custom-call | tf_op jit(solution)/shard_map/merge_heads/pallas_call | solution.py:409

commit v3 on v2

--- a/solution.py
+++ b/solution.py
@@ -122,28 +122,29 @@
     halo = []
 
     def send_halo(n):
-        m = n // 2
-        h, a, p = m // 8, (m // 4) % 2, m % 4
-        part = pl.ds(p * 8, 8)
+        h, a = n // 4, n // 2 % 2
         if n % 2 == 0:
             ref = (kx, vx)[a]
-            src, dst, to = ref.at[h, 2, part], ref.at[h, 0, part], nxt
+            src, dst, to = ref.at[h, 2], ref.at[h, 0], nxt
         else:
-            src, dst, to = (qe, ge)[a].at[h, 0, part], (qn, gn)[a].at[h, part], prv
+            src, dst, to = (qe, ge)[a].at[h, 0], (qn, gn)[a].at[h], prv
         halo.append(remote(src, dst, hssem.at[n], hrsem.at[n], to))
 
     sent = [[], []]
-    for h in range(2):
-        for c in stage[8 * h : 8 * h + 8]:
-            c.wait()
-        for j, to in enumerate(ids):
-            if h == 0:
-                send_halo(j)
-            sent[h].append(
-                remote(st.at[h, to], rc.at[h, me], ssem.at[h, j], rsem.at[h, j], to)
-            )
-        if h == 0:
-            send_halo(31)
+    sent2 = [[], []]
+
+    def send_in(h, j):
+        sent[h].append(
+            remote(st.at[h, ids[j]], rc.at[h, me], ssem.at[h, j], rsem.at[h, j], ids[j])
+        )
+
+    def send_back(h, j):
+        sent2[h].append(
+            remote(st2.at[h, ids[j]], rc2.at[h, me], ssem2.at[h, j], rsem2.at[h, j], ids[j])
+        )
+
+    for n in range(8):
+        send_halo(n)
 
     key_at = lax.broadcasted_iota(jnp.int32, (QB, QB), 0)
     query_at = lax.broadcasted_iota(jnp.int32, (QB, QB), 1)
@@ -191,19 +192,26 @@
         )
         return lse, delta
 
-    @pl.loop(0, 8)
-    def _(step):
-        even_block(step // 4, step % 4 + 4)
+    @pl.loop(4, 8)
+    def _(i):
+        for h in range(2):
+            even_block(h, i)
+
+    for c in halo:
+        c.wait()
+    for h in range(2):
+        for c in stage[8 * h : 8 * h + 8]:
+            c.wait()
+        for j in range(N - 1):
+            send_in(h, j)
 
     def first_row():
-        for c in halo:
-            c.wait_recv()
-
-        @pl.loop(0, 8)
-        def _(step):
-            lse, delta = even_block(step // 4, step % 4)
-            stat[0, pl.ds(step, 1)] = lse
-            stat[1, pl.ds(step, 1)] = delta
+        @pl.loop(0, 4)
+        def _(i):
+            for h in range(2):
+                lse, delta = even_block(h, i)
+                stat[0, pl.ds(h * 4 + i, 1)] = lse
+                stat[1, pl.ds(h * 4 + i, 1)] = delta
 
         return remote(stat, statn, h2s.at[0], h2r.at[0], prv)
 
@@ -228,6 +236,8 @@
                     accv[h, at] += nn(p.astype(BF16), gb)
                     acck[h, at] += nn(ds.astype(BF16), qb)
 
+    stats = first_row()
+
     key_col = key_at // 64
     query_col = query_at // 64
     column = (key_col == query_col) & (key_at % 64 <= query_at % 64)
@@ -266,19 +276,12 @@
             for a in range(3):
                 st2[h, b, a] = tout[a, pl.ds(b * 64, 64)].astype(BF16).reshape(2, W, DH)
 
-    sent2 = [[], []]
     outs = []
 
     def put(src, dst):
         c = pltpu.make_async_copy(src, dst, osem.at[len(outs)])
         c.start()
         outs.append(c)
-
-    def send_back(h, lo, hi):
-        for j in range(lo, hi):
-            sent2[h].append(
-                remote(st2.at[h, ids[j]], rc2.at[h, me], ssem2.at[h, j], rsem2.at[h, j], ids[j])
-            )
 
     for h in range(2):
         mine = pltpu.make_async_copy(st.at[h, me], rc.at[h, me], lsem.at[32 + h])
@@ -289,8 +292,8 @@
         odd_head(h)
         put(st2.at[h, me], rc2.at[h, me])
         if h == 0:
-            send_back(0, 0, N - 1)
-            stats = first_row()
+            for j in range(N - 1):
+                send_back(0, j)
 
     for a in range(2):
         for hh in range(4):
@@ -300,7 +303,8 @@
     scat = []
     for j, to in enumerate(ids):
         scat.append(remote(pgs.at[to], prs.at[me], pss.at[j], prr.at[j], to))
-    send_back(1, 0, 4)
+    for j in range(4):
+        send_back(1, j)
     prs[me] = pgs[me]
     for c in scat:
         c.wait_recv()
@@ -312,7 +316,8 @@
     gath = []
     for j, to in enumerate(ids):
         gath.append(remote(psum, pag.at[me], pas.at[j], par.at[j], to))
-    send_back(1, 4, N - 1)
+    for j in range(4, N - 1):
+        send_back(1, j)
 
     stats.wait_recv()
     next_row()
@@ -331,7 +336,7 @@
         c.wait_recv()
     for c in outs:
         c.wait()
-    for c in halo + sent[0] + sent[1] + [stats] + sent2[0] + sent2[1] + scat + gath:
+    for c in sent[0] + sent[1] + [stats] + sent2[0] + sent2[1] + scat + gath:
         c.wait_send()
 
 
@@ -386,7 +391,7 @@
             pltpu.VMEM((16, DH), BF16),
             dma((34,)),
             dma((2, N - 1)), dma((2, N - 1)),
-            dma((32,)), dma((32,)), dma((1,)), dma((1,)),
+            dma((8,)), dma((8,)), dma((1,)), dma((1,)),
             dma((2, N - 1)), dma((2, N - 1)),
             dma((N - 1,)), dma((N - 1,)), dma((N - 1,)), dma((N - 1,)),
             dma((5,)),
@@ -399,7 +404,7 @@
         prefix_keys,
         prefix_values,
     )
-    steps = 8
+    steps = 2
     wide = pl.BlockSpec((2 * C // steps, 4 * DH), lambda p: (p, 0))
     pre = pl.BlockSpec((NPRE, 4 * DH), lambda p: (0, 0))
     big = jax.ShapeDtypeStruct((2 * C, 4 * DH), BF16)

time: 149 us -> 137 us (0.919)
  Pallas kernels: 148 us -> 136 us
    pallas_call x1, Pallas kernels: 140 us -> 131 us  [body(): pl.pallas_call(kernel, name='strided_backward', out_shape=(jax.ShapeDtype...]
    pallas_call x1, Pallas kernels: 8.2 us -> 5.19 us  [body(): pl.pallas_call(merge, name='merge_heads', grid=(steps,), out_shape=(big,...]
where the time goes in v3:
time: 137 us
  Pallas kernels  136 us (99%)
    pallas_call x1, Pallas kernels, body(): pl.pallas_call(kernel, name='strided_backward', out_shape=(jax.ShapeDtype...  131 us
    pallas_call x1, Pallas kernels, body(): pl.pallas_call(merge, name='merge_heads', grid=(steps,), out_shape=(big,...  5.19 us

profile of v3, /device:TPU:0, one launch (start us, length us, event | category | flops | bytes accessed | tf_op | source)
XLA Modules:
  0.0 136.5 jit_solution(1011757741541919797)
XLA Ops:
  0.6 130.7 %strided_backward.1 = (bf16[2,3,2,32,32,128]{5,4,3,2,1,0:T(8,128)(2,1)}, bf16[2,32,3,2,32,128]{5,4,3,2,1,0:T(8,128)(2,1)}, bf16[32,16,128]{2,1,0:T(8,128)(2,1)}) custom-call(bf16[2,32,32,512]{3,2,1,0:T(8,128)(2,1)} %bitcast.4, bf16[2,32,32,512]{3,2,1,0:T(8,128)(2,1)} %bitcast.5, bf16[2,32,32,512]{3,2,1,0:T(8,128)(2,1)} %bitcast.6, ...), custom_call_target="tpu_custom_call" | custom-call | tf_op jit(solution)/shard_map/strided_backward/pallas_call | solution.py:359
  131.3 5.2 %merge_heads.1 = (bf16[2048,512]{1,0:T(8,128)(2,1)}, bf16[2048,512]{1,0:T(8,128)(2,1)}, bf16[2048,512]{1,0:T(8,128)(2,1)}, f32[64,512]{1,0:T(8,128)}, f32[64,512]{1,0:T(8,128)}) custom-call(bf16[2,3,2,32,32,128]{5,4,3,2,1,0:T(8,128)(2,1)} %get-tuple-element.8.ev, bf16[2,32,3,2,32,128]{5,4,3,2,1,0:T(8,128)(2,1)} %get-tuple-element.9.od, ...), custom_call_target="tpu_custom_call" | custom-call | tf_op jit(solution)/shard_map/merge_heads/pallas_call | solution.py:414

commit v4 on v3

--- a/solution.py
+++ b/solution.py
@@ -17,6 +17,7 @@
 SCALE = 1.0 / math.sqrt(DH)
 LOG2E = SCALE * math.log2(math.e)
 NEG = -1e30
+HALF = 16
 MESH = pl.DeviceIdType.MESH
 F32 = jnp.float32
 BF16 = jnp.bfloat16
@@ -75,32 +76,28 @@
     def lane(hh):
         return pl.ds(hh * DH, DH)
 
-    stage = []
-    n = 0
+    bar = pltpu.get_barrier_semaphore()
+    for i in ids:
+        pl.semaphore_signal(bar, inc=1, device_id={"seq": i}, device_id_type=MESH)
+
+    early, even, stage = [], [], []
+
+    def load(src, dst, group):
+        n = len(early) + len(even) + len(stage)
+        c = pltpu.make_async_copy(src, dst, lsem.at[n])
+        c.start()
+        group.append(c)
+
+    for group in (early, even):
+        for h in range(2):
+            for ref, dst, off in ((k, kx, 1), (v, vx, 1), (q, qe, 0), (g, ge, 0)):
+                r = off if group is early else 1 - off
+                load(ref.at[r, :, :, lane(2 * h)], dst.at[h, r + off], group)
     for h in range(2):
         for a, ref in enumerate((q, k, v, g)):
             for r in range(2):
-                c = pltpu.make_async_copy(
-                    ref.at[r, :, :, lane(2 * h + 1)], st.at[h, :, a, r], lsem.at[n]
-                )
-                c.start()
-                stage.append(c)
-                n += 1
-    even = []
-    for h in range(2):
-        for ref, dst in ((k, kx), (v, vx), (q, qe), (g, ge)):
-            off = 1 if ref is k or ref is v else 0
-            for r in range(2):
-                c = pltpu.make_async_copy(
-                    ref.at[r, :, :, lane(2 * h)], dst.at[h, r + off], lsem.at[n]
-                )
-                c.start()
-                even.append(c)
-                n += 1
-
-    bar = pltpu.get_barrier_semaphore()
-    for i in ids:
-        pl.semaphore_signal(bar, inc=1, device_id={"seq": i}, device_id_type=MESH)
+                load(ref.at[r, :, :, lane(2 * h + 1)], st.at[h, :, a, r], stage)
+
     for hh in range(4):
         pks[hh] = pk[:, hh * DH : (hh + 1) * DH]
         pvs[hh] = pv[:, hh * DH : (hh + 1) * DH]
@@ -117,7 +114,7 @@
         c.start()
         return c
 
-    for c in even:
+    for c in early:
         c.wait()
     halo = []
 
@@ -145,6 +142,8 @@
 
     for n in range(8):
         send_halo(n)
+    for c in even:
+        c.wait()
 
     key_at = lax.broadcasted_iota(jnp.int32, (QB, QB), 0)
     query_at = lax.broadcasted_iota(jnp.int32, (QB, QB), 1)
@@ -199,11 +198,12 @@
 
     for c in halo:
         c.wait()
-    for h in range(2):
-        for c in stage[8 * h : 8 * h + 8]:
-            c.wait()
-        for j in range(N - 1):
-            send_in(h, j)
+    for c in stage:
+        c.wait()
+    for j in range(N - 1):
+        send_in(0, j)
+    for j in range(N - 1):
+        send_in(1, j)
 
     def first_row():
         @pl.loop(0, 4)
@@ -283,6 +283,15 @@
         c.start()
         outs.append(c)
 
+    def even_out():
+        for h in range(2):
+            for a, acc in ((1, acck), (2, accv)):
+                for r in range(2):
+                    part = acc[h, (1 + r) * C : (2 + r) * C]
+                    part = part * SCALE if a == 1 else part
+                    oe[h, a, r] = part.astype(BF16).reshape(N, W, DH)
+            put(oe.at[h], ev.at[h])
+
     for h in range(2):
         mine = pltpu.make_async_copy(st.at[h, me], rc.at[h, me], lsem.at[32 + h])
         mine.start()
@@ -303,7 +312,7 @@
     scat = []
     for j, to in enumerate(ids):
         scat.append(remote(pgs.at[to], prs.at[me], pss.at[j], prr.at[j], to))
-    for j in range(4):
+    for j in range(HALF):
         send_back(1, j)
     prs[me] = pgs[me]
     for c in scat:
@@ -316,18 +325,11 @@
     gath = []
     for j, to in enumerate(ids):
         gath.append(remote(psum, pag.at[me], pas.at[j], par.at[j], to))
-    for j in range(4, N - 1):
+    for j in range(HALF, N - 1):
         send_back(1, j)
-
     stats.wait_recv()
     next_row()
-    for h in range(2):
-        for a, acc in ((1, acck), (2, accv)):
-            for r in range(2):
-                part = acc[h, (1 + r) * C : (2 + r) * C]
-                part = part * SCALE if a == 1 else part
-                oe[h, a, r] = part.astype(BF16).reshape(N, W, DH)
-        put(oe.at[h], ev.at[h])
+    even_out()
 
     for h in range(2):
         for c in sent2[h]:
@@ -383,8 +385,8 @@
             pltpu.VMEM((2, 3, 2, N, W, DH), BF16),
             pltpu.VMEM((2, 8, QB), F32),
             pltpu.VMEM((2, 8, QB), F32),
-            pltpu.VMEM((4, 2 * C, DH), F32),
-            pltpu.VMEM((3, 2 * C, DH), F32),
+            pltpu.VMEM((4, 2 * C + W, DH), F32),
+            pltpu.VMEM((3, 2 * C + W, DH), F32),
             pltpu.VMEM((2, N, 3, 2, W, DH), BF16),
             pltpu.VMEM((N, 16, DH), BF16),
             pltpu.VMEM((N, 16, DH), BF16),

time: 137 us -> 134 us (0.978)
  Pallas kernels: 136 us -> 133 us
    pallas_call x1, Pallas kernels: 131 us -> 127 us  [body(): pl.pallas_call(kernel, name='strided_backward', out_shape=(jax.ShapeDtype...]
where the time goes in v4:
time: 134 us; the launch traced here: 133 us
  Pallas kernels  133 us (99%)
    pallas_call x1, Pallas kernels, body(): pl.pallas_call(kernel, name='strided_backward', out_shape=(jax.ShapeDtype...  127 us
    pallas_call x1, Pallas kernels, body(): pl.pallas_call(merge, name='merge_heads', grid=(steps,), out_shape=(big,...  5.19 us

profile of v4, /device:TPU:0, one launch (start us, length us, event | category | flops | bytes accessed | tf_op | source)
XLA Modules:
  0.0 133.2 jit_solution(5388649467655677267)
XLA Ops:
  0.6 127.3 %strided_backward.1 = (bf16[2,3,2,32,32,128]{5,4,3,2,1,0:T(8,128)(2,1)}, bf16[2,32,3,2,32,128]{5,4,3,2,1,0:T(8,128)(2,1)}, bf16[32,16,128]{2,1,0:T(8,128)(2,1)}) custom-call(bf16[2,32,32,512]{3,2,1,0:T(8,128)(2,1)} %bitcast.4, bf16[2,32,32,512]{3,2,1,0:T(8,128)(2,1)} %bitcast.5, bf16[2,32,32,512]{3,2,1,0:T(8,128)(2,1)} %bitcast.6, ...), custom_call_target="tpu_custom_call" | custom-call | tf_op jit(solution)/shard_map/strided_backward/pallas_call | solution.py:361
  128.0 5.2 %merge_heads.1 = (bf16[2048,512]{1,0:T(8,128)(2,1)}, bf16[2048,512]{1,0:T(8,128)(2,1)}, bf16[2048,512]{1,0:T(8,128)(2,1)}, f32[64,512]{1,0:T(8,128)}, f32[64,512]{1,0:T(8,128)}) custom-call(bf16[2,3,2,32,32,128]{5,4,3,2,1,0:T(8,128)(2,1)} %get-tuple-element.8.ev, bf16[2,32,3,2,32,128]{5,4,3,2,1,0:T(8,128)(2,1)} %get-tuple-element.9.od, ...), custom_call_target="tpu_custom_call" | custom-call | tf_op jit(solution)/shard_map/merge_heads/pallas_call | solution.py:416

commit v5 on v4

--- a/solution.py
+++ b/solution.py
@@ -271,6 +271,7 @@
                 for cc in range(4):
                     tout[a, pl.ds(cg * 4 + cc, 64, stride=W), :] = val[cc * 64 : cc * 64 + 64]
 
+    def odd_pack(h):
         @pl.loop(0, N, unroll=2)
         def _(b):
             for a in range(3):
@@ -299,8 +300,9 @@
         for c in sent[h]:
             c.wait_recv()
         odd_head(h)
-        put(st2.at[h, me], rc2.at[h, me])
         if h == 0:
+            odd_pack(0)
+            put(st2.at[0, me], rc2.at[0, me])
             for j in range(N - 1):
                 send_back(0, j)
 
@@ -312,6 +314,8 @@
     scat = []
     for j, to in enumerate(ids):
         scat.append(remote(pgs.at[to], prs.at[me], pss.at[j], prr.at[j], to))
+    odd_pack(1)
+    put(st2.at[1, me], rc2.at[1, me])
     for j in range(HALF):
         send_back(1, j)
     prs[me] = pgs[me]

time: 134 us -> 133 us (level)
  no operation moved by 1% of the time
where the time goes in v5:
time: 133 us
  Pallas kernels  132 us (99%)
    pallas_call x1, Pallas kernels, body(): pl.pallas_call(kernel, name='strided_backward', out_shape=(jax.ShapeDtype...  127 us
    pallas_call x1, Pallas kernels, body(): pl.pallas_call(merge, name='merge_heads', grid=(steps,), out_shape=(big,...  5.19 us

profile of v5, /device:TPU:0, one launch (start us, length us, event | category | flops | bytes accessed | tf_op | source)
XLA Modules:
  0.0 133.1 jit_solution(13603238204109906794)
XLA Ops:
  0.6 127.3 %strided_backward.1 = (bf16[2,3,2,32,32,128]{5,4,3,2,1,0:T(8,128)(2,1)}, bf16[2,32,3,2,32,128]{5,4,3,2,1,0:T(8,128)(2,1)}, bf16[32,16,128]{2,1,0:T(8,128)(2,1)}) custom-call(bf16[2,32,32,512]{3,2,1,0:T(8,128)(2,1)} %bitcast.4, bf16[2,32,32,512]{3,2,1,0:T(8,128)(2,1)} %bitcast.5, bf16[2,32,32,512]{3,2,1,0:T(8,128)(2,1)} %bitcast.6, ...), custom_call_target="tpu_custom_call" | custom-call | tf_op jit(solution)/shard_map/strided_backward/pallas_call | solution.py:365
  127.9 5.2 %merge_heads.1 = (bf16[2048,512]{1,0:T(8,128)(2,1)}, bf16[2048,512]{1,0:T(8,128)(2,1)}, bf16[2048,512]{1,0:T(8,128)(2,1)}, f32[64,512]{1,0:T(8,128)}, f32[64,512]{1,0:T(8,128)}) custom-call(bf16[2,3,2,32,32,128]{5,4,3,2,1,0:T(8,128)(2,1)} %get-tuple-element.8.ev, bf16[2,32,3,2,32,128]{5,4,3,2,1,0:T(8,128)(2,1)} %get-tuple-element.9.od, ...), custom_call_target="tpu_custom_call" | custom-call | tf_op jit(solution)/shard_map/merge_heads/pallas_call | solution.py:420
